TPU v7x, 256 devices: a whole 4x4x8 slice. The times are simulated.
256 devices in a mesh: row: 8 (over z), col: 32 (over x, y, core).
Axes of the slice: x: 4, y: 4, z: 8, core: 2. Of those that a mesh axis runs over, the one named last changes fastest.
Arguments:
- source_points: bfloat16 [64, 32768], P('col', 'row'), may hold values from -1 to 1
- target_points: bfloat16 [64, 131072], P('row', 'col'), may hold values from -0.8984375 to 0.8984375
- target_potential: float32 [131072], P('col'), may hold values from -2 to 8
Outputs:
- source_new: float32 [32768], P('row')
- target_new: float32 [131072], P('col')
All inputs are finite; a program needn't handle non-finite values.
Results may differ from a plain program's by a relative error of at most 0.0003.
Values may be sent and summed in bfloat16 or wider, within the bound.
No kernel may reach another device: no remote copies, remote signals or barrier semaphores. Data moves between devices by JAX's collectives and lax.ppermute only.
A program may use at most 64 MiB of HBM per device.

v0:
```python
import math

import jax
import jax.numpy as jnp
from jax import lax
from jax.sharding import PartitionSpec as P

EPS = 0.05


def on_device(source_points, target_points, target_potential):
    src_full = lax.all_gather(source_points, "col", axis=0, tiled=True)
    tgt_full = lax.all_gather(target_points, "row", axis=0, tiled=True)
    src_norm = jnp.sum(jnp.square(src_full.astype(jnp.float32)), axis=0)
    tgt_norm = jnp.sum(jnp.square(tgt_full.astype(jnp.float32)), axis=0)
    src_rows = src_full.shape[1]
    tgt_rows = tgt_full.shape[1]
    tgt_total = tgt_rows * lax.axis_size("col")
    src_total = src_rows * lax.axis_size("row")
    block_rows = math.gcd(src_rows, 512)
    block_count = src_rows // block_rows
    src_blocks = src_full.reshape(src_full.shape[0], block_count, block_rows).transpose(1, 0, 2)
    norm_blocks = src_norm.reshape(block_count, block_rows)

    def cost_of(src_block, norm_block):
        cross_term = jnp.dot(src_block.T, tgt_full, preferred_element_type=jnp.float32)
        return norm_block[:, None] + tgt_norm[None, :] - 2.0 * cross_term

    def first_pass(pieces):
        src_block, norm_block = pieces
        scores = (target_potential[None, :] - cost_of(src_block, norm_block)) / EPS
        row_peak = jnp.max(scores, axis=1)
        row_total = jnp.sum(jnp.exp(scores - row_peak[:, None]), axis=1)
        return (row_peak, row_total)

    local_peak, local_total = lax.map(first_pass, (src_blocks, norm_blocks))
    local_peak = local_peak.reshape(src_rows)
    local_total = local_total.reshape(src_rows)
    glob_peak = lax.pmax(local_peak, "col")
    glob_total = lax.psum(local_total * jnp.exp(local_peak - glob_peak), "col")
    source_new = -EPS * (glob_peak + jnp.log(glob_total)) + EPS * math.log(tgt_total)
    pot_blocks = source_new.reshape(block_count, block_rows)

    def second_pass(carry, pieces):
        col_peak, col_total = carry
        src_block, norm_block, pot_block = pieces
        scores = (pot_block[:, None] - cost_of(src_block, norm_block)) / EPS
        new_peak = jnp.maximum(col_peak, jnp.max(scores, axis=0))
        new_total = col_total * jnp.exp(col_peak - new_peak) + jnp.sum(
            jnp.exp(scores - new_peak[None, :]), axis=0
        )
        return ((new_peak, new_total), None)

    start = (jnp.full((tgt_rows,), -jnp.inf, jnp.float32), jnp.zeros((tgt_rows,), jnp.float32))
    (col_peak, col_total), _ = lax.scan(second_pass, start, (src_blocks, norm_blocks, pot_blocks))
    full_peak = lax.pmax(col_peak, "row")
    full_total = lax.psum(col_total * jnp.exp(col_peak - full_peak), "row")
    target_new = -EPS * (full_peak + jnp.log(full_total)) + EPS * math.log(src_total)
    return (source_new, target_new)


def solution(mesh):
    return jax.shard_map(
        on_device,
        mesh=mesh,
        in_specs=(P("col", "row"), P("row", "col"), P("col")),
        out_specs=(P("row"), P("col")),
        check_vma=False,
    )
```

profile of v0, /device:TPU:32, one launch (start us, length us, event | category | flops | bytes accessed | tf_op | source)
XLA Modules:
  0.0 424.7 jit_solution(16547241271619193929)
XLA Ops:
  0.7 28.3 %all_gather.7 = bf16[64,4096]{1,0:T(8,128)(2,1)S(1)} all-gather(bf16[8,4096]{1,0:T(8,128)(2,1)} %param.8), channel_id=1, replica_groups=mesh['row'=8,'col'=32] {'row'}, dimensions={0}, use_global_device_ids=true | all-gather | bytes 589824 | tf_op jit(solution)/shard_map/all_gather | solution.py:13
  29.1 25.1 %all-gather = bf16[32,2,4096]{2,1,0:T(2,128)(2,1)S(1)} all-gather(bf16[1,2,4096]{2,1,0:T(2,128)(2,1)} %bitcast.50), channel_id=1, replica_groups=mesh['row'=8,'col'=32] {'col'}, dimensions={0}, use_global_device_ids=true | all-gather | bytes 540672 | tf_op jit(solution)/shard_map/all_gather | solution.py:12
  55.3 34.5 %while.25 = (s32[]{:T(128)}, f32[8,512]{1,0:T(8,128)S(1)}, f32[8,512]{1,0:T(8,128)S(1)}, f32[4096]{0:T(1024)}, f32[8,512]{1,0:T(8,128)S(1)}, /*index=5*/f32[4096...) while((s32[]{:T(128)}, f32[8,512]{1,0:T(8,128)S(1)}, ...), condition=%wide.region_5.6_spmd, body=%wide.region_2.5_spmd.sunk | while | flops 285211648 | bytes 17420412 | solution.py:36
  55.3 2.9 fusion.17
  59.6 2.9 fusion.17
  64.0 2.9 fusion.17
  68.3 2.9 fusion.17
  72.6 2.9 fusion.17
  76.9 2.9 fusion.17
  81.2 2.9 fusion.17
  85.5 2.9 fusion.17
  89.8 126.4 %pmax.14 = f32[4096]{0:T(1024)S(1)} all-reduce(f32[4096]{0:T(1024)S(1)} %bitcast.44), channel_id=1, replica_groups=mesh['row'=8,'col'=32] {'col'}, use_global_device_ids=true, to_apply=%region_6.7 | all-reduce | flops 4096 | bytes 32768 | tf_op jit(solution)/shard_map/pmax | solution.py:39
  216.2 123.8 %psum.14 = f32[4096]{0:T(1024)S(1)} all-reduce(f32[4096]{0:T(1024)S(1)} %exponential_multiply_fusion.1), channel_id=1, replica_groups=mesh['row'=8,'col'=32] {'col'}, use_global_device_ids=true, to_apply=%region_7.8 | all-reduce | flops 4096 | bytes 32768 | tf_op jit(solution)/shard_map/psum | solution.py:40
  340.6 27.6 %while.26 = (s32[]{:T(128)}, f32[4096]{0:T(1024)S(1)}, f32[4096]{0:T(1024)S(1)}, f32[8,512]{1,0:T(8,128)S(1)}, f32[8,512]{1,0:T(8,128)S(1)}, /*index=5*/f32[4096...) while((s32[]{:T(128)}, f32[4096]{0:T(1024)S(1)}, ...), condition=%wide.region_11.12_spmd.clone, body=%wide.region_8.11_spmd.clone.sunk | while | flops 285233152 | bytes 17608832 | solution.py:55
  340.6 2.0 fusion.19
  342.7 1.3 exponential_reduce_fusion.5
  344.1 2.0 fusion.19
  346.1 1.3 exponential_reduce_fusion.5
  347.5 2.0 fusion.19
  349.6 1.3 exponential_reduce_fusion.5
  351.0 2.0 fusion.19
  353.0 1.3 exponential_reduce_fusion.5
  354.4 2.0 fusion.19
  356.5 1.3 exponential_reduce_fusion.5
  357.9 2.0 fusion.19
  359.9 1.3 exponential_reduce_fusion.5
  361.3 2.0 fusion.19
  363.4 1.3 exponential_reduce_fusion.5
  364.8 2.0 fusion.19
  366.8 1.3 exponential_reduce_fusion.5
  368.2 26.8 %pmax.15 = f32[4096]{0:T(1024)S(1)} all-reduce(f32[4096]{0:T(1024)S(1)} %get-tuple-element.90), channel_id=1, replica_groups=mesh['row'=8,'col'=32] {'row'}, use_global_device_ids=true, to_apply=%region_12.13 | all-reduce | flops 4096 | bytes 32768 | tf_op jit(solution)/shard_map/pmax | solution.py:56
  395.1 29.0 %psum.15 = f32[4096]{0:T(1024)S(1)} all-reduce(f32[4096]{0:T(1024)S(1)} %exponential_multiply_fusion), channel_id=1, replica_groups=mesh['row'=8,'col'=32] {'row'}, use_global_device_ids=true, to_apply=%region_13.14 | all-reduce | flops 4096 | bytes 32768 | tf_op jit(solution)/shard_map/psum | solution.py:57
  (82 shorter events, 14.1 us)
Async XLA Ops:
  340.0 0.6 copy-start
where the time goes:
time: 426 us; the launch traced here: 425 us
  blocking collectives  359 us (84%)
  matrix products  39.2 us (9%)
  other arithmetic  22.4 us (5%)
    pmax x1, blocking collectives, on_device(): glob_peak = lax.pmax(local_peak, 'col')  126 us
    psum x1, blocking collectives, on_device(): glob_total = lax.psum(local_total * jnp.exp(local_peak - glob_peak), 'col')  124 us
    dot_general x16, matrix products, cost_of(): jnp.dot(src_block.T, tgt_full, preferred_element_type=jnp.float32)  39.2 us
    psum x1, blocking collectives, on_device(): full_total = lax.psum(col_total * jnp.exp(col_peak - full_peak), 'row')  29 us
    all_gather x1, blocking collectives, on_device(): tgt_full = lax.all_gather(target_points, 'row', axis=0, tiled=True)  28.3 us
    pmax x1, blocking collectives, on_device(): full_peak = lax.pmax(col_peak, 'row')  26.8 us
    all_gather x1, blocking collectives, on_device(): src_full = lax.all_gather(source_points, 'col', axis=0, tiled=True)  25.1 us
    reduce_sum x8, other arithmetic, second_pass(): jnp.sum(jnp.exp(scores - new_peak[None, :]), axis=0)  10.6 us

commit v1 on v0

v1 whole, which is shorter than its diff:
```python
import functools
import math

import jax
import jax.numpy as jnp
from jax import lax
from jax.experimental import pallas as pl
from jax.experimental.pallas import tpu as pltpu
from jax.sharding import PartitionSpec as P

EPS = 0.05
LN2 = math.log(2.0)
KAPPA = 1.0 / (EPS * LN2)
ROWS = 128
LANES = 512


def split3(v):
    hi = v.astype(jnp.bfloat16)
    rest = v - hi.astype(jnp.float32)
    mid = rest.astype(jnp.bfloat16)
    low = (rest - mid.astype(jnp.float32)).astype(jnp.bfloat16)
    return hi, mid, low


def fill_operands(streamed, fixed, bias, lhs, rhs):
    d, n = streamed.shape
    hi, mid, low = split3(bias)
    row = lax.broadcasted_iota(jnp.int32, (d, n), 0)
    rows = jnp.where(row == 0, hi.astype(jnp.float32), 0.0)
    rows = jnp.where(row == 1, mid.astype(jnp.float32), rows)
    rows = jnp.where(row == 2, low.astype(jnp.float32), rows)
    points = streamed.astype(jnp.float32)
    lhs[:, : 2 * d] = jnp.concatenate([points, rows], axis=0).T.astype(jnp.bfloat16)
    lhs[:, 2 * d :] = jnp.concatenate([points, points], axis=0).T.astype(jnp.bfloat16)
    hi, mid, low = split3(fixed.astype(jnp.float32) * (2.0 * KAPPA))
    rhs[:d] = hi
    rhs[d : 2 * d] = jnp.where(row < 3, 1.0, 0.0).astype(jnp.bfloat16)
    rhs[2 * d : 3 * d] = mid
    rhs[3 * d :] = low


def column_lse(lhs, rhs, out):
    n = lhs.shape[0]

    def block(step, carry):
        lanes = pl.ds(pl.multiple_of(step * LANES, LANES), LANES)
        weights = rhs[:, lanes]
        peak = jnp.full((8, LANES), -jnp.inf, jnp.float32)
        total = jnp.zeros((8, LANES), jnp.float32)
        for start in range(0, n, ROWS):
            scores = jnp.dot(lhs[start : start + ROWS, :], weights, preferred_element_type=jnp.float32)
            scores = scores.reshape(ROWS // 8, 8, LANES)
            new_peak = jnp.maximum(peak, scores.max(0))
            total = total * jnp.exp2(peak - new_peak) + jnp.exp2(scores - new_peak[None]).sum(0)
            peak = new_peak
        top = peak.max(0, keepdims=True)
        out[:, lanes] = top + jnp.log2((total * jnp.exp2(peak - top)).sum(0, keepdims=True))
        return carry

    lax.fori_loop(0, rhs.shape[1] // LANES, block, 0)


def square_norm(points):
    return jnp.sum(jnp.square(points.astype(jnp.float32)), axis=0, keepdims=True)


def lse_of(parts):
    top = parts.max(0, keepdims=True)
    return top + jnp.log2(jnp.exp2(parts - top).sum(0, keepdims=True))


def first_kernel(src, tgt, pot, out, lhs, rhs):
    bias = KAPPA * (pot[...] - square_norm(tgt[...]))
    fill_operands(tgt[...], src[...], bias, lhs, rhs)
    column_lse(lhs, rhs, out)


def second_kernel(tgt_total, parts, src, tgt, new, out, lhs, rhs):
    bias = math.log2(tgt_total) - lse_of(parts[...])
    new[...] = square_norm(src[...]) + EPS * LN2 * bias
    fill_operands(src[...], tgt[...], bias, lhs, rhs)
    column_lse(lhs, rhs, out)


def gathered(x, axis):
    size = lax.axis_size(axis)
    whole = jnp.broadcast_to(x[None], (size,) + x.shape)
    return lax.all_to_all(whole, axis, 0, 0, tiled=True)


def on_device(source_points, target_points, target_potential):
    n_src = source_points.shape[1]
    n_tgt = target_points.shape[1]
    tgt_total = n_tgt * lax.axis_size("col")
    src_total = n_src * lax.axis_size("row")
    src = gathered(source_points, "col").reshape(-1, n_src)
    tgt = gathered(target_points, "row").reshape(-1, n_tgt)
    depth = 4 * src.shape[0]
    params = pltpu.CompilerParams(vmem_limit_bytes=48 * 2**20)
    partial = pl.pallas_call(
        first_kernel,
        out_shape=jax.ShapeDtypeStruct((1, n_src), jnp.float32),
        scratch_shapes=[pltpu.VMEM((n_tgt, depth), jnp.bfloat16), pltpu.VMEM((depth, n_src), jnp.bfloat16)],
        compiler_params=params,
        name="first_pass",
    )(src, tgt, target_potential.reshape(1, n_tgt))
    parts = gathered(partial.reshape(n_src), "col")
    source_new, partial = pl.pallas_call(
        functools.partial(second_kernel, tgt_total),
        out_shape=[jax.ShapeDtypeStruct((1, n_src), jnp.float32), jax.ShapeDtypeStruct((1, n_tgt), jnp.float32)],
        scratch_shapes=[pltpu.VMEM((n_src, depth), jnp.bfloat16), pltpu.VMEM((depth, n_tgt), jnp.bfloat16)],
        compiler_params=params,
        name="second_pass",
    )(parts, src, tgt)
    parts = gathered(partial.reshape(n_tgt), "row")
    target_new = square_norm(tgt) - EPS * LN2 * lse_of(parts) + EPS * math.log(src_total)
    return source_new.reshape(n_src), target_new.reshape(n_tgt)


def solution(mesh):
    return jax.shard_map(
        on_device,
        mesh=mesh,
        in_specs=(P("col", "row"), P("row", "col"), P("col")),
        out_specs=(P("row"), P("col")),
        check_vma=False,
    )
```

time: 426 us -> 111 us (0.26)
  the two profiles are of different devices: /device:TPU:32 before, /device:TPU:1 now
where the time goes in v1:
time: 111 us; the launch traced here: 110 us
  blocking collectives  35.4 us (32%)
  Pallas kernels  30.7 us (28%)
  waiting for transfers between devices  27.2 us (25%)
  starting transfers between devices  11.6 us (10%)
  local copies, waits for them, and re-layouts  3.7 us (3%)
    all_to_all x2, blocking collectives, gathered(): return lax.all_to_all(whole, axis, 0, 0, tiled=True)  35.4 us
    all_to_all x2, waiting for transfers between devices, gathered(): return lax.all_to_all(whole, axis, 0, 0, tiled=True)  27.2 us
    pallas_call x1, Pallas kernels, on_device(): pl.pallas_call(first_kernel, out_shape=jax.ShapeDtypeStruct((1, n_src), j...  15.4 us
    pallas_call x1, Pallas kernels, on_device(): pl.pallas_call(functools.partial(second_kernel, tgt_total), out_shape=[ja...  15.3 us
    all_to_all x2, starting transfers between devices, gathered(): return lax.all_to_all(whole, axis, 0, 0, tiled=True)  11.6 us
    broadcast_in_dim x4, local copies, waits for them, and re-layouts, gathered(): whole = jnp.broadcast_to(x[None], (size,) + x.shape)  3.18 us
  transfers between devices with their start and end apart: 2, of which 2 were waited for; matrix products, arithmetic and copies ran while one was open for 0% of the time, Pallas kernels for 0%

profile of v1, /device:TPU:1, one launch (start us, length us, event | category | flops | bytes accessed | tf_op | source)
XLA Modules:
  0.0 110.2 jit_solution(403741479738997763)
XLA Ops:
  0.6 1.2 %broadcast_in_dim.8 = bf16[32,2,4096]{2,1,0:T(2,128)(2,1)S(1)} broadcast(bf16[2,4096]{1,0:T(2,128)(2,1)} %param.3), dimensions={1,2} | broadcast | bytes 540672 | tf_op jit(solution)/shard_map/broadcast_in_dim | solution.py:88
  1.8 0.0 copy-start.1
  1.8 20.1 %all_to_all.27 = bf16[32,2,4096]{2,1,0:T(2,128)(2,1)S(1)} all-to-all(bf16[32,2,4096]{2,1,0:T(2,128)(2,1)S(1)} %broadcast_in_dim.8), channel_id=1, replica_groups=mesh['row'=8,'col'=32] {'col'}, dimensions={0} | all-to-all | bytes 1048576 | tf_op jit(solution)/shard_map/all_to_all | solution.py:89
  22.0 0.0 copy-done.1
  22.0 0.8 broadcast_in_dim.9
  22.8 8.2 %all-to-all-start.1 = ((bf16[8,8,4096]{2,1,0:T(8,128)(2,1)}), bf16[8,8,4096]{2,1,0:T(8,128)(2,1)S(1)}, u32[]{:S(2)}, u32[]{:S(2)}) async-start(bf16[8,8,4096]{2,1,0:T(8,128)(2,1)} %broadcast_in_dim.9), calls=%async_computation.1 | async-start | bytes 1048576 | tf_op jit(solution)/shard_map/all_to_all | solution.py:89
  31.0 0.0 copy-start
  31.0 0.2 reshape.41.src
  31.2 17.9 %all-to-all-done.1 = bf16[8,8,4096]{2,1,0:T(8,128)(2,1)S(1)} async-done(((bf16[8,8,4096]{2,1,0:T(8,128)(2,1)}), bf16[8,8,4096]{2,1,0:T(8,128)(2,1)S(1)}, u32[]{:S(2)}, u32[]{:S(2)}) %all-to-all-start.1) | async-done | bytes 524320 | tf_op jit(solution)/shard_map/all_to_all | solution.py:89
  49.1 0.0 copy-done
  49.1 15.4 %first_pass.1 = f32[1,4096]{1,0:T(1,128)S(1)} custom-call(bf16[64,4096]{1,0:T(8,128)(2,1)S(1)} %reshape.41.src, bf16[64,4096]{1,0:T(8,128)(2,1)S(1)} %bitcast.16, f32[1,4096]{1,0:T(1,128)S(1)} %bitcast.20), custom_call_target="tpu_custom_call" | custom-call | tf_op jit(solution)/shard_map/first_pass/pallas_call | solution.py:101
  64.4 0.5 broadcast_in_dim.10
  64.9 15.2 %all_to_all.28 = f32[32,1,4096]{2,1,0:T(1,128)S(1)} all-to-all(f32[32,1,4096]{2,1,0:T(1,128)S(1)} %broadcast_in_dim.10), channel_id=1, replica_groups=mesh['row'=8,'col'=32] {'col'}, dimensions={0} | all-to-all | bytes 1048576 | tf_op jit(solution)/shard_map/all_to_all | solution.py:89
  80.1 0.3 copy.11
  80.4 15.3 %second_pass.1 = (f32[1,4096]{1,0:T(1,128)}, f32[1,4096]{1,0:T(1,128)S(1)}) custom-call(f32[32,4096]{1,0:T(8,128)S(1)} %bitcast.18, bf16[64,4096]{1,0:T(8,128)(2,1)S(1)} %reshape.41.src, bf16[64,4096]{1,0:T(8,128)(2,1)S(1)} %bitcast.17), custom_call_target="tpu_custom_call" | custom-call | tf_op jit(solution)/shard_map/second_pass/pallas_call | solution.py:109
  95.8 0.7 broadcast_in_dim.11
  96.5 3.4 %all-to-all-start.3 = ((f32[8,1,4096]{2,1,0:T(1,128)}), f32[8,1,4096]{2,1,0:T(1,128)S(1)}, u32[]{:S(2)}, u32[]{:S(2)}) async-start(f32[8,1,4096]{2,1,0:T(1,128)} %broadcast_in_dim.11), calls=%async_computation.3 | async-start | bytes 262144 | tf_op jit(solution)/shard_map/all_to_all | solution.py:89
  99.8 0.1 multiply_reduce_fusion
  100.0 9.4 %all-to-all-done.3 = f32[8,1,4096]{2,1,0:T(1,128)S(1)} async-done(((f32[8,1,4096]{2,1,0:T(1,128)}), f32[8,1,4096]{2,1,0:T(1,128)S(1)}, u32[]{:S(2)}, u32[]{:S(2)}) %all-to-all-start.3) | async-done | bytes 131104 | tf_op jit(solution)/shard_map/all_to_all | solution.py:89
  109.4 0.1 reduce_max.9
  109.5 0.1 fusion.2
  109.6 0.6 subtract_add_fusion
Async XLA Ops:
  1.8 20.2 %copy-start.1 = (bf16[8,4096]{1,0:T(8,128)(2,1)S(1)}, bf16[8,4096]{1,0:T(8,128)(2,1)}, u32[]{:S(2)}) copy-start(bf16[8,4096]{1,0:T(8,128)(2,1)} %param.4) | copy-start | bytes 196612
  22.8 26.3 %all-to-all-start.1 = ((bf16[8,8,4096]{2,1,0:T(8,128)(2,1)}), bf16[8,8,4096]{2,1,0:T(8,128)(2,1)S(1)}, u32[]{:S(2)}, u32[]{:S(2)}) async-start(bf16[8,8,4096]{2,1,0:T(8,128)(2,1)} %broadcast_in_dim.9), calls=%async_computation.1 | async-start | bytes 1048576 | tf_op jit(solution)/shard_map/all_to_all | solution.py:89
  31.0 18.1 %copy-start = (f32[4096]{0:T(1024)S(1)}, f32[4096]{0:T(1024)}, u32[]{:S(2)}) copy-start(f32[4096]{0:T(1024)} %param.5) | copy-start | bytes 49156
  96.5 12.9 %all-to-all-start.3 = ((f32[8,1,4096]{2,1,0:T(1,128)}), f32[8,1,4096]{2,1,0:T(1,128)S(1)}, u32[]{:S(2)}, u32[]{:S(2)}) async-start(f32[8,1,4096]{2,1,0:T(1,128)} %broadcast_in_dim.11), calls=%async_computation.3 | async-start | bytes 262144 | tf_op jit(solution)/shard_map/all_to_all | solution.py:89
